TPU v7x, 32 devices: a whole 2x2x4 slice. The times are simulated.
32 devices in a mesh: dp: 8 (over z, x), own: 4 (over y, core).
Axes of the slice: x: 2, y: 2, z: 4, core: 2. Of those that a mesh axis runs over, the one named last changes fastest.
Arguments:
- grads: bfloat16 [8, 4, 1024, 1024], P('dp', 'own'), may hold values from -6 to 6
- left: float32 [4, 1024, 1024], P('own', 'dp')
- right: float32 [4, 1024, 1024], P('own', 'dp')
- root_left: bfloat16 [4, 1024, 1024], P('own', 'dp'), as said below
- root_right: bfloat16 [4, 1024, 1024], P('own', 'dp')
- first: float32 [4, 1024, 1024], P('own', 'dp'), may hold values from -1.1 to 1.1
- second: float32 [4, 1024, 1024], P('own', 'dp'), may hold values from 0.003 to 0.05
- owner: int32 [4], replicated, may hold values from 0 to 3, each once
Outputs:
- new_left: float32 [4, 1024, 1024], P('own', 'dp')
- new_right: float32 [4, 1024, 1024], P('own', 'dp')
- new_first: float32 [4, 1024, 1024], P('own', 'dp')
- new_second: float32 [4, 1024, 1024], P('own', 'dp')
- direction: bfloat16 [4, 1024, 1024], P(None, 'dp')
Inputs may be any that keep to these rules, and one draw needn't show every extreme that they name: owner is a permutation of 0 to 3. root_left and root_right are symmetric.
All inputs are finite; a program needn't handle non-finite values.
Results may differ from a plain program's by a relative error of at most 0.015.
Values may be sent and summed in bfloat16 or wider, within the bound.
A program may use at most 64 MiB of HBM per device.

v0:
```python
import jax
import jax.numpy as jnp
from jax import lax
from jax.sharding import PartitionSpec as P


def statistics(left, right, gradient, grad_rows, begin, row_count):
    outer_left = lax.dot_general(
        grad_rows, gradient, (((1,), (1,)), ((), ())), preferred_element_type=jnp.float32
    )
    columns = lax.dynamic_slice_in_dim(gradient, begin, row_count, 1)
    outer_right = lax.dot_general(
        columns, gradient, (((0,), (0,)), ((), ())), preferred_element_type=jnp.float32
    )
    return (0.95 * left[0] + 0.05 * outer_left, 0.95 * right[0] + 0.05 * outer_right)


def precondition(root_left, root_right, gradient):
    inner = jnp.dot(root_left[0], gradient, preferred_element_type=jnp.float32).astype(jnp.bfloat16)
    return jnp.dot(
        inner,
        lax.all_gather(root_right, "dp", axis=1, tiled=True)[0],
        preferred_element_type=jnp.float32,
    )


def body(grads, left, right, root_left, root_right, first, second, owner):
    replicas = lax.axis_size("dp")
    row_count = left.shape[1]
    begin = lax.axis_index("dp") * row_count
    partial_value = grads[0, 0].astype(jnp.float32)
    summed = lax.psum_scatter(
        partial_value.astype(jnp.bfloat16), "dp", scatter_dimension=0, tiled=True
    ).astype(jnp.float32)
    grad_rows = (summed / replicas).astype(jnp.bfloat16)
    gradient = lax.all_gather(grad_rows, "dp", axis=0, tiled=True)
    updated_left, updated_right = statistics(left, right, gradient, grad_rows, begin, row_count)
    precond = precondition(root_left, root_right, gradient)
    grad_value = grad_rows.astype(jnp.float32)
    moment_one = 0.9 * first[0] + 0.1 * grad_value
    moment_two = 0.999 * second[0] + 0.001 * grad_value * grad_value
    adam = moment_one / (jnp.sqrt(moment_two) + 1e-08)
    adam_sq, precond_sq = lax.psum((jnp.sum(adam * adam), jnp.sum(precond * precond)), "dp")
    scale = jnp.sqrt(adam_sq) / (jnp.sqrt(precond_sq) + 1e-06)
    update = (precond * scale).astype(jnp.bfloat16)
    gathered = lax.all_gather(update[None], "own", axis=0, tiled=True)
    direction = jnp.take(gathered, owner, axis=0)
    return (updated_left[None], updated_right[None], moment_one[None], moment_two[None], direction)


def solution(mesh):
    return jax.shard_map(
        body,
        mesh=mesh,
        in_specs=(
            P("dp", "own", None, None),
            P("own", "dp", None),
            P("own", "dp", None),
            P("own", "dp", None),
            P("own", "dp", None),
            P("own", "dp", None),
            P("own", "dp", None),
            P(),
        ),
        out_specs=(
            P("own", "dp", None),
            P("own", "dp", None),
            P("own", "dp", None),
            P("own", "dp", None),
            P(None, "dp", None),
        ),
        check_vma=False,
    )
```

profile of v0, /device:TPU:0, one launch (start us, length us, event | category | flops | bytes accessed | tf_op | source)
XLA Modules:
  0.0 233.2 jit_solution(10221159409172053029)
XLA Ops:
  7.2 0.0 copy-start
  7.2 0.0 copy-start.3
  7.2 0.0 copy-start.4
  7.2 0.0 reduce-scatter.2.cloned.1.call-start
  7.2 0.7 reduce-scatter.2.cloned.1.call-update
  7.9 0.0 all-gather.7.cloned.1.call-start
  8.0 0.7 all-gather.7.cloned.1.call-update
  8.7 0.0 all-gather.5.cloned.1.call-start
  8.7 73.7 %reduce-scatter.2.cloned.1.call-done = bf16[128,1024]{1,0:T(8,128)(2,1)} async-done(((bf16[1024,1024]{1,0:T(8,128)(2,1)}), bf16[128,1024]{1,0:T(8,128)(2,1)}) %reduce-scatter.2.cloned.1.call-update) | async-done | bytes 262160 | tf_op jit(solution)/shard_map/reduce_scatter | solution.py:32
  82.4 0.0 copy-done.3
  82.4 0.0 copy-done.4
  82.4 2.8 %multiply_reduce_fusion.1 = (f32[]{:T(128)}, f32[1,128,1024]{2,1,0:T(8,128)}, f32[1,128,1024]{2,1,0:T(8,128)}, bf16[128,1024]{1,0:T(8,128)(2,1)}) fusion(f32[1,128,1024]{2,1,0:T(8,128)S(1)} %copy-done.3, f32[1,128,1024]{2,1,0:T(8,128)S(1)} %copy-done.4, bf16[128,1024]{1,0:T(8,128)(2,1)} %reduce-scatter.2.cloned.1.call-done), kind=kLoop, calls=%fused_computation.17 | loop fusion | flops 1966079 | bytes 2621444 | tf_op jit(solution)/shard_map/reduce_sum | solution.py:43
  85.2 0.0 all-gather.5.cloned.1.call-update
  85.3 0.0 copy-start.6
  85.3 0.0 all-gather.9.cloned.1.call-start
  85.3 47.6 %all-gather.7.cloned.1.call-done = bf16[1,1024,1024]{2,1,0:T(8,128)(2,1)} async-done(((bf16[1,128,1024]{2,1,0:T(8,128)(2,1)}), bf16[1,1024,1024]{2,1,0:T(8,128)(2,1)}) %all-gather.7.cloned.1.call-update) | async-done | bytes 2097168 | tf_op jit(solution)/shard_map/all_gather | solution.py:22
  132.9 50.5 %all-gather.5.cloned.1.call-done = bf16[1024,1024]{1,0:T(8,128)(2,1)} async-done(((bf16[128,1024]{1,0:T(8,128)(2,1)}), bf16[1024,1024]{1,0:T(8,128)(2,1)}) %all-gather.5.cloned.1.call-update) | async-done | bytes 2097168 | tf_op jit(solution)/shard_map/all_gather | solution.py:36
  183.4 0.0 copy-done
  183.4 4.5 %multiply_reduce_fusion = (f32[]{:T(128)}, f32[128,1024]{1,0:T(8,128)S(1)}) fusion(bf16[1,1024,1024]{2,1,0:T(8,128)(2,1)} %all-gather.7.cloned.1.call-done, bf16[1024,1024]{1,0:T(8,128)(2,1)} %all-gather.5.cloned.1.call-done, bf16[1,128,1024]{2,1,0:T(8,128)(2,1)S(1)} %copy-done), kind=kOutput, calls=%fused_computation.16 | convolution fusion | flops 537264128 | bytes 4980740 | tf_op jit(solution)/shard_map/dot_general | solution.py:20
  187.9 19.5 %all-reduce = (f32[]{:T(128)}, f32[]{:T(128)}) all-reduce(f32[]{:T(128)} %get-tuple-element.7, f32[]{:T(128)} %get-tuple-element.11), channel_id=1, replica_groups=mesh['dp'=8,'own'=4] {'dp'}, use_global_device_ids=true, to_apply=%region_2.0 | all-reduce | flops 2 | bytes 16 | tf_op jit(solution)/shard_map/psum | solution.py:43
  208.8 0.0 copy-start.2
  208.8 0.7 multiply_convert_fusion
  209.6 0.0 all-gather.9.cloned.1.call-update
  209.6 0.0 copy-done.6
  209.7 0.0 copy-done.1
  209.7 2.4 %fusion.3 = f32[1,128,1024]{2,1,0:T(8,128)} fusion(bf16[1024,1024]{1,0:T(8,128)(2,1)S(1)} %copy-done.1, f32[1,128,1024]{2,1,0:T(8,128)} %param.10, s32[]{:T(128)S(6)} %select_n.12), kind=kOutput, calls=%fused_computation.5 | convolution fusion | flops 268828672 | bytes 3407876 | tf_op jit(solution)/shard_map/dot_general | solution.py:12
  212.1 0.0 copy-done.2
  212.1 0.0 copy-done.5
  212.1 1.6 fusion.5
  213.7 10.0 %all-gather.9.cloned.1.call-done = bf16[512,1024]{1,0:T(8,128)(2,1)} async-done(((bf16[128,1024]{1,0:T(8,128)(2,1)}), bf16[512,1024]{1,0:T(8,128)(2,1)}) %all-gather.9.cloned.1.call-update) | async-done | bytes 1048592 | tf_op jit(solution)/shard_map/all_gather | solution.py:46
  223.7 1.8 gather_fusion
  225.6 1.1 broadcast_select_fusion
  (5 shorter events, 0.0 us)
Async XLA Ops:
  7.2 176.2 %copy-start = (bf16[1,128,1024]{2,1,0:T(8,128)(2,1)S(1)}, bf16[1,128,1024]{2,1,0:T(8,128)(2,1)}, u32[]{:S(2)}) copy-start(bf16[1,128,1024]{2,1,0:T(8,128)(2,1)} %param.11) | copy-start | bytes 786436
  7.2 75.2 %copy-start.3 = (f32[1,128,1024]{2,1,0:T(8,128)S(1)}, f32[1,128,1024]{2,1,0:T(8,128)}, u32[]{:S(2)}) copy-start(f32[1,128,1024]{2,1,0:T(8,128)} %param.13) | copy-start | bytes 1572868
  7.2 75.2 %copy-start.4 = (f32[1,128,1024]{2,1,0:T(8,128)S(1)}, f32[1,128,1024]{2,1,0:T(8,128)}, u32[]{:S(2)}) copy-start(f32[1,128,1024]{2,1,0:T(8,128)} %param.14) | copy-start | bytes 1572868
  7.2 75.2 %reduce-scatter.2.cloned.1.call-start = ((), (), s32[]{:S(2)}) async-start(), calls=%async_computation.1 | async-start | bytes 2359296 | tf_op jit(solution)/shard_map/reduce_scatter | solution.py:32
  7.9 124.9 %all-gather.7.cloned.1.call-start = ((), (), s32[]{:S(2)}) async-start(), calls=%async_computation.3 | async-start | bytes 2359296 | tf_op jit(solution)/shard_map/all_gather | solution.py:22
  8.7 174.7 %all-gather.5.cloned.1.call-start = ((), (), s32[]{:S(2)}) async-start(), calls=%async_computation.2 | async-start | bytes 2359296 | tf_op jit(solution)/shard_map/all_gather | solution.py:36
  85.3 124.4 %copy-start.6 = (s32[4]{0:T(128)S(1)}, s32[4]{0:T(128)}, u32[]{:S(2)}) copy-start(s32[4]{0:T(128)} %param.15) | copy-start | bytes 52
  85.3 138.5 %all-gather.9.cloned.1.call-start = ((), (), s32[]{:S(2)}) async-start(), calls=%async_computation.4 | async-start | bytes 1310720 | tf_op jit(solution)/shard_map/all_gather | solution.py:46
  183.4 26.3 %copy-start.1 = (bf16[1024,1024]{1,0:T(8,128)(2,1)S(1)}, bf16[1024,1024]{1,0:T(8,128)(2,1)}, u32[]{:S(2)}) copy-start(bf16[1024,1024]{1,0:T(8,128)(2,1)} %all-gather.5.cloned.1.call-done) | copy-start | bytes 6291460
  208.8 3.2 %copy-start.2 = (bf16[128,1024]{1,0:T(8,128)(2,1)S(1)}, bf16[128,1024]{1,0:T(8,128)(2,1)}, u32[]{:S(2)}) copy-start(bf16[128,1024]{1,0:T(8,128)(2,1)} %reduce-scatter.2.cloned.1.call-done) | copy-start | bytes 786436
  209.6 2.5 %copy-start.5 = (f32[1,128,1024]{2,1,0:T(8,128)S(1)}, f32[1,128,1024]{2,1,0:T(8,128)}, u32[]{:S(2)}) copy-start(f32[1,128,1024]{2,1,0:T(8,128)} %param.9) | copy-start | bytes 1572868
Sparse Core Ops, SparseCore 0:
  11.6 70.8 reduce-scatter.1
  84.6 48.2 all-gather.6
  135.6 47.7 all-gather.4
  209.7 13.9 all-gather.8
where the time goes:
time: 233 us
  waiting for transfers between devices  183 us (79%)
  blocking collectives  19.5 us (8%)
  between operations  15.3 us (7%)
  matrix products  8.49 us (4%)
  other arithmetic  4.7 us (2%)
    reduce_scatter x1, waiting for transfers between devices, body(): lax.psum_scatter(partial_value.astype(jnp.bfloat16), 'dp', scatter_dimens...  73.7 us
    all_gather x1, waiting for transfers between devices, body(): gradient = lax.all_gather(grad_rows, 'dp', axis=0, tiled=True)  50.5 us
    all_gather x1, waiting for transfers between devices, precondition(): lax.all_gather(root_right, 'dp', axis=1, tiled=True)[0]  47.6 us
    psum x1, blocking collectives, body(): lax.psum((jnp.sum(adam * adam), jnp.sum(precond * precond)), 'dp')  19.5 us
    all_gather x1, waiting for transfers between devices, body(): gathered = lax.all_gather(update[None], 'own', axis=0, tiled=True)  10 us
  transfers between devices with their start and end apart: 4, of which 4 were waited for; matrix products, arithmetic and copies ran while one was open for 3% of the time, Pallas kernels for 0%

commit v1 on v0

v1 whole, which is shorter than its diff:
```python
import functools

import jax
import jax.numpy as jnp
from jax import lax
from jax.experimental import pallas as pl
from jax.experimental.pallas import tpu as pltpu
from jax.sharding import PartitionSpec as P

MESH = pl.DeviceIdType.MESH
F32 = jnp.float32
BF16 = jnp.bfloat16
LANES = 128
DEPTH = 3


def remote(src, dst, send, recv, axis, to):
    return pltpu.make_async_remote_copy(
        src_ref=src, dst_ref=dst, send_sem=send, recv_sem=recv,
        device_id={axis: to}, device_id_type=MESH,
    )


def kernel(n, owners, halves, cuts, grads, left, right, root_left, root_right, first, second, owner,
           new_left, new_right, new_first, new_second, direction,
           mine, xbuf, ubuf, dbuf, total, g, window, full, left_v, right_v, rl_v, first_v, second_v,
           inner, turned, product, parts, tile, stats, scales,
           load_sem, store_sem, xs, xr, us, ur, ds, dr, gxs, gxr, gus, gur, gds, gdr,
           rxs, rxr, rus, rur, rds, rdr, ps, pr, cs, cr, ss, sr, ts, tr):
    me = lax.axis_index("dp")
    own = lax.axis_index("own")
    size = g.shape[0]
    rows = left_v.shape[0]
    depth_z = n // 2
    z, x = me // 2, me % 2
    partner, above, below = z * 2 + 1 - x, me + 2, me - 2
    pairs = owners // 2
    pair, core = own // 2, own % 2
    part = rows // halves
    groups = size // LANES
    span = window.shape[1] // LANES
    has_above, has_below = z < depth_z - 1, z > 0

    load_mine = pltpu.make_async_copy(grads.at[:, x], mine, load_sem.at[0])
    loads = [
        pltpu.make_async_copy(src.at[0], dst, load_sem.at[i + 1])
        for i, (src, dst) in enumerate(
            ((root_left, rl_v), (first, first_v), (second, second_v), (left, left_v), (right, right_v)))
    ]
    my_rows = pl.ds(pl.multiple_of(me * rows, rows), rows)
    group = (me * rows) // LANES
    loads_rr = [
        pltpu.make_async_copy(
            root_right.at[0, :, pl.ds(pl.multiple_of(((group + k) % groups) * LANES, LANES), LANES)],
            window.at[my_rows, pl.ds(k * LANES, LANES)], load_sem.at[6 + k])
        for k in range(span)
    ]
    for copy in loads_rr:
        copy.start()
    load_mine.start()
    for copy in loads:
        copy.start()

    barrier = pltpu.get_barrier_semaphore()
    for k in range(1, n):
        pl.semaphore_signal(barrier, inc=1, device_id={"dp": (me + k) % n}, device_id_type=MESH)
    for k in range(1, owners):
        pl.semaphore_signal(barrier, inc=1, device_id={"own": (own + k) % owners}, device_id_type=MESH)
    pl.semaphore_wait(barrier, n + owners - 2)

    low = (z < depth_z // 2).astype(jnp.int32)

    def dest(s):
        if s == depth_z - 1:
            return z
        t = depth_z - 1 - s
        down_order = t - (z >= t).astype(jnp.int32)
        up_order = s + (z <= s).astype(jnp.int32)
        return low * down_order + (1 - low) * up_order

    steps = [(s, h) for s in range(depth_z) for h in range(halves)]

    def sub(h):
        return pl.ds(h * part, part)

    def send_x(i):
        s, h = steps[i]
        t = dest(s)
        return remote(grads.at[t, 1 - x, sub(h)], xbuf.at[t, sub(h)], xs.at[i], xr.at[i], "dp", partner)

    def send_up(t, h):
        return remote(mine.at[t, sub(h)], ubuf.at[t, sub(h)], us.at[t, h], ur.at[t, h], "dp", above)

    def send_down(t, h):
        return remote(mine.at[t, sub(h)], dbuf.at[t, sub(h)], ds.at[t, h], dr.at[t, h], "dp", below)

    def block(t, column, h):
        return g.at[pl.ds(pl.multiple_of((2 * t + column) * rows + h * part, part), part)]

    def gat_x(t, h):
        return remote(block(t, x, h), block(t, x, h), gxs.at[t, h], gxr.at[t, h], "dp", partner)

    def gat_up(t, h):
        return remote(block(t, x, h), block(t, x, h), gus.at[t, h], gur.at[t, h], "dp", above)

    def gat_down(t, h):
        return remote(block(t, x, h), block(t, x, h), gds.at[t, h], gdr.at[t, h], "dp", below)

    def wblock(stream, t):
        column = x if stream == 0 else 1 - x
        return window.at[pl.ds(pl.multiple_of((2 * t + column) * rows, rows), rows)]

    def root_x():
        return remote(wblock(0, z), wblock(0, z), rxs.at[0], rxr.at[0], "dp", partner)

    def root_up(stream, t):
        w = wblock(stream, t)
        return remote(w, w, rus.at[stream, t], rur.at[stream, t], "dp", above)

    def root_down(stream, t):
        w = wblock(stream, t)
        return remote(w, w, rds.at[stream, t], rdr.at[stream, t], "dp", below)

    def root_event(stream, k):
        if k == 0:
            if stream == 1:
                root_x().wait_recv()

            @pl.when(has_above)
            def _():
                root_up(stream, z).start()

            @pl.when(has_below)
            def _():
                root_down(stream, z).start()
            return

        @pl.when(z >= k)
        def _():
            root_up(stream, z - k).wait_recv()

            @pl.when(has_above)
            def _():
                root_up(stream, z - k).start()

        @pl.when(z + k < depth_z)
        def _():
            root_down(stream, z + k).wait_recv()

            @pl.when(has_below)
            def _():
                root_down(stream, z + k).start()

    for i in range(min(DEPTH, len(steps))):
        send_x(i).start()
    for copy in loads_rr:
        copy.wait()
    root_event(0, 0)
    load_mine.wait()

    events = {}
    for k in range(1, depth_z):
        events.setdefault(k - 1, []).append((0, k))
    for k in range(depth_z):
        events.setdefault(k + 1, []).append((1, k))

    for i, (s, h) in enumerate(steps):
        t = dest(s)
        send_x(i).wait_recv()
        if i + DEPTH < len(steps):
            send_x(i + DEPTH).start()
        if i == 0:
            root_x().start()
        rs = sub(h)
        acc = mine[t, rs].astype(F32) + xbuf[t, rs].astype(F32)
        if s < depth_z - 1:
            up, down = t > z, t < z

            @pl.when(up & has_below)
            def _():
                send_up(t, h).wait_recv()
                mine[t, rs] = (acc + ubuf[t, rs].astype(F32)).astype(BF16)

            @pl.when(down & has_above)
            def _():
                send_down(t, h).wait_recv()
                mine[t, rs] = (acc + dbuf[t, rs].astype(F32)).astype(BF16)

            @pl.when((up & (z == 0)) | (down & (z == depth_z - 1)))
            def _():
                mine[t, rs] = acc.astype(BF16)

            @pl.when(up)
            def _():
                send_up(t, h).start()

            @pl.when(down)
            def _():
                send_down(t, h).start()
        else:
            total[rs] = acc

            @pl.when(has_below)
            def _():
                send_up(t, h).wait_recv()
                total[rs] = total[rs] + ubuf[t, rs].astype(F32)

            @pl.when(has_above)
            def _():
                send_down(t, h).wait_recv()
                total[rs] = total[rs] + dbuf[t, rs].astype(F32)

            g[pl.ds(pl.multiple_of(me * rows + h * part, part), part)] = (total[rs] / n).astype(BF16)
            gat_x(z, h).start()

            @pl.when(has_above)
            def _():
                gat_up(z, h).start()

            @pl.when(has_below)
            def _():
                gat_down(z, h).start()
        if h == halves - 1:
            for event in events.pop(s, ()):
                root_event(*event)

    for copy in loads:
        copy.wait()
    value = g[my_rows].astype(F32)
    one = 0.9 * first_v[...] + 0.1 * value
    two = 0.999 * second_v[...] + 0.001 * value * value
    first_v[...] = one
    second_v[...] = two
    adam = one / (jnp.sqrt(two) + 1e-08)
    adam_sq = jnp.sum(jnp.sum(adam * adam, axis=0, keepdims=True), axis=1, keepdims=True)
    stores = [
        pltpu.make_async_copy(src, dst.at[0], store_sem.at[i])
        for i, (src, dst) in enumerate(
            ((first_v, new_first), (second_v, new_second), (left_v, new_left), (right_v, new_right)))
    ]
    stores[0].start()
    stores[1].start()

    for k in range(1, depth_z):
        for h in range(halves):
            @pl.when(z >= k)
            def _():
                gat_up(z - k, h).wait_recv()
                gat_x(z - k, h).start()

                @pl.when(has_above)
                def _():
                    gat_up(z - k, h).start()

            @pl.when(z + k < depth_z)
            def _():
                gat_down(z + k, h).wait_recv()
                gat_x(z + k, h).start()

                @pl.when(has_below)
                def _():
                    gat_down(z + k, h).start()
        for event in events.pop(depth_z - 1 + k, ()):
            root_event(*event)

    def rebuild(i, carry):
        r = pl.ds(pl.multiple_of(i * LANES, LANES), LANES)
        for k in range(span):
            c = pl.ds(pl.multiple_of(((i + k) % groups) * LANES, LANES), LANES)
            piece = window[r, pl.ds(k * LANES, LANES)]
            full[r, c] = piece
            if k and 2 * k < groups:
                full[c, r] = piece.T
        return carry

    lax.fori_loop(0, groups, rebuild, 0)

    for t in range(depth_z):
        for h in range(halves):
            gat_x(t, h).wait_recv()

    width = 256

    def tile_of(i):
        return pl.ds(pl.multiple_of(i * width, width), width)

    def inner_step(i, carry):
        c = tile_of(i)
        inner[:, c] = jnp.dot(rl_v[...], g[:, c], preferred_element_type=F32).astype(BF16)
        return carry

    lax.fori_loop(0, size // width, inner_step, 0)

    def parts_at(slot, cut):
        w = size // cuts
        return parts.at[slot, :, pl.ds(cut * w, w)]

    def to_pair(k, cut):
        here = parts_at(own, cut)
        return remote(here, here, ps.at[k, cut], pr.at[k, cut], "own", ((pair + k) % pairs) * 2 + core)

    def to_core(k, cut):
        here = parts_at(((pair + pairs - k) % pairs) * 2 + core, cut)
        return remote(here, here, cs.at[k, cut], cr.at[k, cut], "own", pair * 2 + 1 - core)

    precond_sq = jnp.zeros((1, 1), F32)
    for cut in range(cuts):
        w = size // cuts
        for j in range(w // width):
            c = pl.ds(cut * w + j * width, width)
            precond = jnp.dot(inner[...], full[:, c], preferred_element_type=F32)
            parts[own, :, c] = precond.astype(BF16)
            precond_sq += jnp.sum(
                jnp.sum(precond * precond, axis=0, keepdims=True), axis=1, keepdims=True)
        for k in range(1, pairs):
            to_pair(k, cut).start()
        to_core(0, cut).start()

    line = lax.broadcasted_iota(jnp.int32, tile.shape, 0)
    tile[...] = jnp.where(line == 0, adam_sq, precond_sq)
    stats[me] = tile[...]

    def norm_to(k):
        return remote(tile, stats.at[me], ss.at[k], sr.at[k], "dp", (me + k) % n)

    for k in range(1, n):
        norm_to(k).start()

    def left_step(i, carry):
        c = tile_of(i)
        outer = lax.dot_general(g[my_rows], g[c, :], (((1,), (1,)), ((), ())), preferred_element_type=F32)
        left_v[:, c] = 0.95 * left_v[:, c] + 0.05 * outer
        return carry

    lax.fori_loop(0, size // width, left_step, 0)
    stores[2].start()

    for k in range(1, n):
        norm_to(k).wait_recv()
    sums = stats[0]
    for i in range(1, n):
        sums = sums + stats[i]
    scale = jnp.sqrt(sums[0:1]) / (jnp.sqrt(sums[1:2]) + 1e-06)
    scales[own] = jnp.broadcast_to(scale, scales.shape[1:])

    def scale_to(k):
        return remote(scales.at[own], scales.at[own], ts.at[k], tr.at[k], "own", (own + k) % owners)

    for k in range(1, owners):
        scale_to(k).start()

    for cut in range(cuts):
        for k in range(1, pairs):
            to_pair(k, cut).wait_recv()
            to_core(k, cut).start()

    aligned = pl.ds(pl.multiple_of(group * LANES, LANES), LANES)

    def turn_step(i, carry):
        r = pl.ds(pl.multiple_of(i * LANES, LANES), LANES)
        turned[:, r] = g[r, aligned].T
        return carry

    lax.fori_loop(0, groups, turn_step, 0)
    offset = pl.ds(pl.multiple_of(me * rows - group * LANES, 8), rows)

    def right_step(i, carry):
        c = tile_of(i)
        product[...] = jnp.dot(turned[...], g[:, c], preferred_element_type=F32)
        right_v[:, c] = 0.95 * right_v[:, c] + 0.05 * product[offset]
        return carry

    lax.fori_loop(0, size // width, right_step, 0)
    stores[3].start()

    for k in range(1, owners):
        scale_to(k).wait_recv()
    for cut in range(cuts):
        for k in range(pairs):
            to_core(k, cut).wait_recv()
    for b in range(owners):
        direction[b] = (parts[owner[b]].astype(F32) * scales[owner[b]][0:1, 0:1]).astype(BF16)

    for i, (s, h) in enumerate(steps):
        send_x(i).wait_send()
        gat_x(s, h).wait_send()
    for t in range(depth_z):
        for h in range(halves):
            @pl.when(z < t)
            def _():
                send_up(t, h).wait_send()

            @pl.when(z > t)
            def _():
                send_down(t, h).wait_send()

            @pl.when((z >= t) & has_above)
            def _():
                gat_up(t, h).wait_send()

            @pl.when((z <= t) & has_below)
            def _():
                gat_down(t, h).wait_send()
        for stream in range(2):
            @pl.when((z >= t) & has_above)
            def _():
                root_up(stream, t).wait_send()

            @pl.when((z <= t) & has_below)
            def _():
                root_down(stream, t).wait_send()
    root_x().wait_send()
    for k in range(1, n):
        norm_to(k).wait_send()
    for k in range(1, owners):
        scale_to(k).wait_send()
    for cut in range(cuts):
        for k in range(pairs):
            to_core(k, cut).wait_send()
            if k:
                to_pair(k, cut).wait_send()
    for copy in stores:
        copy.wait()


def body(n, owners, grads, left, right, root_left, root_right, first, second, owner):
    rows, size = left.shape[1:]
    line = n // 2
    halves = max(1, rows // 64)
    cuts = 2
    pairs = owners // 2
    span = size // LANES // 2 + 1
    sem = pltpu.SemaphoreType.DMA
    stat = jax.ShapeDtypeStruct((1, rows, size), F32)
    anywhere = pl.BlockSpec(memory_space=pl.ANY)
    return pl.pallas_call(
        functools.partial(kernel, n, owners, halves, cuts),
        out_shape=(stat, stat, stat, stat, jax.ShapeDtypeStruct((owners, rows, size), BF16)),
        in_specs=[anywhere] * 7 + [pl.BlockSpec(memory_space=pltpu.SMEM)],
        out_specs=(anywhere,) * 4 + (pl.BlockSpec(memory_space=pltpu.VMEM),),
        scratch_shapes=[
            *[pltpu.VMEM((line, rows, size), BF16)] * 4,
            pltpu.VMEM((rows, size), F32),
            pltpu.VMEM((size, size), BF16),
            pltpu.VMEM((size, span * LANES), BF16),
            pltpu.VMEM((size, size), BF16),
            pltpu.VMEM((rows, size), F32),
            pltpu.VMEM((rows, size), F32),
            pltpu.VMEM((rows, size), BF16),
            pltpu.VMEM((rows, size), F32),
            pltpu.VMEM((rows, size), F32),
            pltpu.VMEM((rows, size), BF16),
            pltpu.VMEM((LANES, size), BF16),
            pltpu.VMEM((LANES, 256), F32),
            pltpu.VMEM((owners, rows, size), BF16),
            pltpu.VMEM((8, LANES), F32),
            pltpu.VMEM((n, 8, LANES), F32),
            pltpu.VMEM((owners, 8, LANES), F32),
            sem((6 + span,)), sem((4,)),
            sem((line * halves,)), sem((line * halves,)),
            *[sem((line, halves))] * 10,
            sem((1,)), sem((1,)),
            *[sem((2, line))] * 4,
            *[sem((pairs, cuts))] * 4,
            sem((n,)), sem((n,)), sem((owners,)), sem((owners,)),
        ],
        compiler_params=pltpu.CompilerParams(
            collective_id=0, has_side_effects=True, vmem_limit_bytes=40 * 1024 * 1024),
        cost_estimate=pl.CostEstimate(
            flops=8 * rows * size * size, bytes_accessed=24 * rows * size, transcendentals=rows * size),
    )(grads.reshape(line, 2, rows, size), left, right, root_left, root_right, first, second, owner)


def solution(mesh):
    split = P("own", "dp", None)
    return jax.shard_map(
        functools.partial(body, mesh.shape["dp"], mesh.shape["own"]),
        mesh=mesh,
        in_specs=(P("dp", "own", None, None),) + (split,) * 6 + (P(),),
        out_specs=(split,) * 4 + (P(None, "dp", None),),
        check_vma=False,
    )
```

time: 233 us -> 92.5 us (0.40)
  waiting for transfers between devices: 183 us -> 0 us
  Pallas kernels: 0 us -> 78.9 us
  blocking collectives: 19.5 us -> 0 us
  between operations: 15.3 us -> 0.66 us
  local copies, waits for them, and re-layouts: 1.87 us -> 12.4 us
  matrix products: 8.49 us -> 0 us
  other arithmetic: 4.7 us -> 0 us
    all_gather x3 -> x0, waiting for transfers between devices: 108 us -> none  [the longest x1 50.5 us: body(): gradient = lax.all_gather(grad_rows, 'dp', axis=0, tiled=True)]
    pallas_call x0 -> x1, Pallas kernels: none -> 78.9 us  [body(): pl.pallas_call(functools.partial(kernel, n, owners, halves, cuts), out_sh...]
    reduce_scatter x1 -> x0, waiting for transfers between devices: 73.7 us -> none  [body(): lax.psum_scatter(partial_value.astype(jnp.bfloat16), 'dp', scatter_dimens...]
    psum x1 -> x0, blocking collectives: 19.5 us -> none  [body(): lax.psum((jnp.sum(adam * adam), jnp.sum(precond * precond)), 'dp')]
    unnamed x14 -> x21, local copies, waits for them, and re-layouts: 0.04 us -> 12.4 us
    dot_general x3 -> x0, matrix products: 8.49 us -> none  [the longest x1 4.47 us: precondition(): jnp.dot(inner, lax.all_gather(root_right, 'dp', axis=1, tiled=True)[0], p...]
    reduce_sum x1 -> x0, other arithmetic: 2.8 us -> none  [body(): jnp.sum(adam * adam)]
  transfers between devices with their start and end apart: 4 -> 0, of which waited for: 4 -> 0; matrix products, arithmetic and copies ran while one was open for 3% -> 0% of each run, Pallas kernels for 0% -> 0%
where the time goes in v1:
time: 92.5 us; the launch traced here: 92 us
  Pallas kernels  78.9 us (85%)
  local copies, waits for them, and re-layouts  12.4 us (13%)
    pallas_call x1, Pallas kernels, body(): pl.pallas_call(functools.partial(kernel, n, owners, halves, cuts), out_sh...  78.9 us
    unnamed x21, local copies, waits for them, and re-layouts  12.4 us

profile of v1, /device:TPU:0, one launch (start us, length us, event | category | flops | bytes accessed | tf_op | source)
XLA Modules:
  0.0 92.0 jit_solution(10896602391549045542)
XLA Ops:
  0.6 0.0 copy-start
  0.6 1.6 %copy-done = bf16[1,1,1024,1024]{3,2,1,0:T(8,128)(2,1)S(1)} copy-done((bf16[1,1,1024,1024]{3,2,1,0:T(8,128)(2,1)S(1)}, bf16[1,1,1024,1024]{3,2,1,0:T(8,128)(2,1)}, u32[]{:S(2)}) %copy-start) | copy-done | bytes 2097176
  2.2 0.0 copy-start.1
  2.2 1.0 %copy-done.1 = f32[1,128,1024]{2,1,0:T(8,128)S(1)} copy-done((f32[1,128,1024]{2,1,0:T(8,128)S(1)}, f32[1,128,1024]{2,1,0:T(8,128)}, u32[]{:S(2)}) %copy-start.1) | copy-done | bytes 524312
  3.3 0.0 copy-start.2
  3.3 1.0 %copy-done.2 = f32[1,128,1024]{2,1,0:T(8,128)S(1)} copy-done((f32[1,128,1024]{2,1,0:T(8,128)S(1)}, f32[1,128,1024]{2,1,0:T(8,128)}, u32[]{:S(2)}) %copy-start.2) | copy-done | bytes 524312
  4.3 0.0 copy-start.3
  4.3 1.0 %copy-done.3 = f32[1,128,1024]{2,1,0:T(8,128)S(1)} copy-done((f32[1,128,1024]{2,1,0:T(8,128)S(1)}, f32[1,128,1024]{2,1,0:T(8,128)}, u32[]{:S(2)}) %copy-start.3) | copy-done | bytes 524312
  5.4 0.0 copy-start.4
  5.4 1.0 %copy-done.4 = f32[1,128,1024]{2,1,0:T(8,128)S(1)} copy-done((f32[1,128,1024]{2,1,0:T(8,128)S(1)}, f32[1,128,1024]{2,1,0:T(8,128)}, u32[]{:S(2)}) %copy-start.4) | copy-done | bytes 524312
  6.4 0.0 copy-start.5
  6.4 0.9 %copy-done.5 = bf16[1,128,1024]{2,1,0:T(8,128)(2,1)S(1)} copy-done((bf16[1,128,1024]{2,1,0:T(8,128)(2,1)S(1)}, bf16[1,128,1024]{2,1,0:T(8,128)(2,1)}, u32[]{:S(2)}) %copy-start.5) | copy-done | bytes 262168
  7.3 0.0 copy-start.6
  7.3 0.9 %copy-done.6 = bf16[1,128,1024]{2,1,0:T(8,128)(2,1)S(1)} copy-done((bf16[1,128,1024]{2,1,0:T(8,128)(2,1)S(1)}, bf16[1,128,1024]{2,1,0:T(8,128)(2,1)}, u32[]{:S(2)}) %copy-start.6) | copy-done | bytes 262168
  8.3 0.0 copy-start.7
  8.3 0.7 copy-done.7
  9.0 78.9 %shard_map.119 = (f32[1,128,1024]{2,1,0:T(8,128)S(1)}, f32[1,128,1024]{2,1,0:T(8,128)S(1)}, f32[1,128,1024]{2,1,0:T(8,128)S(1)}, f32[1,128,1024]{2,1,0:T(8,128)S(1)}, bf16[4,128,1024]{2,1,0:T(8,128)(2,1)S(1)}) custom-call(bf16[4,2,128,1024]{3,2,1,0:T(8,128)(2,1)S(1)} %bitcast.1, f32[1,128,1024]{2,1,0:T(8,128)S(1)} %copy-done.1, ...), custom_call_target="tpu_custom_call" | custom-call | flops 1073741824 | bytes 3145728 | tf_op jit(solution)/shard_map/pallas_call | solution.py:436
  87.9 0.8 copy.18
  88.7 0.8 copy.19
  89.5 0.8 copy.20
  90.3 0.8 copy.21
  91.1 1.0 %copy.22 = bf16[4,128,1024]{2,1,0:T(8,128)(2,1)} copy(bf16[4,128,1024]{2,1,0:T(8,128)(2,1)S(1)} %get-tuple-element.14) | data formatting | bytes 2097152
Async XLA Ops:
  0.6 1.6 %copy-start = (bf16[1,1,1024,1024]{3,2,1,0:T(8,128)(2,1)S(1)}, bf16[1,1,1024,1024]{3,2,1,0:T(8,128)(2,1)}, u32[]{:S(2)}) copy-start(bf16[1,1,1024,1024]{3,2,1,0:T(8,128)(2,1)} %param.8) | copy-start | bytes 6291460
  2.2 1.0 %copy-start.1 = (f32[1,128,1024]{2,1,0:T(8,128)S(1)}, f32[1,128,1024]{2,1,0:T(8,128)}, u32[]{:S(2)}) copy-start(f32[1,128,1024]{2,1,0:T(8,128)} %left.1) | copy-start | bytes 1572868
  3.3 1.0 %copy-start.2 = (f32[1,128,1024]{2,1,0:T(8,128)S(1)}, f32[1,128,1024]{2,1,0:T(8,128)}, u32[]{:S(2)}) copy-start(f32[1,128,1024]{2,1,0:T(8,128)} %right.1) | copy-start | bytes 1572868
  4.3 1.0 %copy-start.3 = (f32[1,128,1024]{2,1,0:T(8,128)S(1)}, f32[1,128,1024]{2,1,0:T(8,128)}, u32[]{:S(2)}) copy-start(f32[1,128,1024]{2,1,0:T(8,128)} %first.1) | copy-start | bytes 1572868
  5.4 1.0 %copy-start.4 = (f32[1,128,1024]{2,1,0:T(8,128)S(1)}, f32[1,128,1024]{2,1,0:T(8,128)}, u32[]{:S(2)}) copy-start(f32[1,128,1024]{2,1,0:T(8,128)} %second.1) | copy-start | bytes 1572868
  6.4 0.9 %copy-start.5 = (bf16[1,128,1024]{2,1,0:T(8,128)(2,1)S(1)}, bf16[1,128,1024]{2,1,0:T(8,128)(2,1)}, u32[]{:S(2)}) copy-start(bf16[1,128,1024]{2,1,0:T(8,128)(2,1)} %root_left.1) | copy-start | bytes 786436
  7.3 0.9 %copy-start.6 = (bf16[1,128,1024]{2,1,0:T(8,128)(2,1)S(1)}, bf16[1,128,1024]{2,1,0:T(8,128)(2,1)}, u32[]{:S(2)}) copy-start(bf16[1,128,1024]{2,1,0:T(8,128)(2,1)} %root_right.1) | copy-start | bytes 786436
  8.3 0.7 copy-start.7

commit v2 on v1

--- a/solution.py
+++ b/solution.py
@@ -23,10 +23,10 @@
 
 def kernel(n, owners, halves, cuts, grads, left, right, root_left, root_right, first, second, owner,
            new_left, new_right, new_first, new_second, direction,
-           mine, xbuf, ubuf, dbuf, total, g, window, full, left_v, right_v, rl_v, first_v, second_v,
-           inner, turned, product, parts, tile, stats, scales,
+           mine, xbuf, ubuf, dbuf, total, g, right_rows, left_v, right_v, rl_v, first_v, second_v,
+           inner, turned, product, parts, away, tile, stats, scales,
            load_sem, store_sem, xs, xr, us, ur, ds, dr, gxs, gxr, gus, gur, gds, gdr,
-           rxs, rxr, rus, rur, rds, rdr, ps, pr, cs, cr, ss, sr, ts, tr):
+           rxs, rxr, rus, rur, rds, rdr, axs, axr, ps, pr, cs, cr, ss, sr, ts, tr):
     me = lax.axis_index("dp")
     own = lax.axis_index("own")
     size = g.shape[0]
@@ -38,25 +38,21 @@
     pair, core = own // 2, own % 2
     part = rows // halves
     groups = size // LANES
-    span = window.shape[1] // LANES
     has_above, has_below = z < depth_z - 1, z > 0
+
+    def root_rows(t):
+        return right_rows.at[pl.ds(pl.multiple_of(t * rows, rows), rows)]
 
     load_mine = pltpu.make_async_copy(grads.at[:, x], mine, load_sem.at[0])
     loads = [
         pltpu.make_async_copy(src.at[0], dst, load_sem.at[i + 1])
         for i, (src, dst) in enumerate(
-            ((root_left, rl_v), (first, first_v), (second, second_v), (left, left_v), (right, right_v)))
+            ((root_left, rl_v.at[pl.ds(0, rows)]), (first, first_v), (second, second_v), (left, left_v), (right, right_v)))
     ]
     my_rows = pl.ds(pl.multiple_of(me * rows, rows), rows)
     group = (me * rows) // LANES
-    loads_rr = [
-        pltpu.make_async_copy(
-            root_right.at[0, :, pl.ds(pl.multiple_of(((group + k) % groups) * LANES, LANES), LANES)],
-            window.at[my_rows, pl.ds(k * LANES, LANES)], load_sem.at[6 + k])
-        for k in range(span)
-    ]
-    for copy in loads_rr:
-        copy.start()
+    load_rr = pltpu.make_async_copy(root_right.at[0], root_rows(z), load_sem.at[6])
+    load_rr.start()
     load_mine.start()
     for copy in loads:
         copy.start()
@@ -106,70 +102,55 @@
     def gat_down(t, h):
         return remote(block(t, x, h), block(t, x, h), gds.at[t, h], gdr.at[t, h], "dp", below)
 
-    def wblock(stream, t):
-        column = x if stream == 0 else 1 - x
-        return window.at[pl.ds(pl.multiple_of((2 * t + column) * rows, rows), rows)]
-
     def root_x():
-        return remote(wblock(0, z), wblock(0, z), rxs.at[0], rxr.at[0], "dp", partner)
-
-    def root_up(stream, t):
-        w = wblock(stream, t)
-        return remote(w, w, rus.at[stream, t], rur.at[stream, t], "dp", above)
-
-    def root_down(stream, t):
-        w = wblock(stream, t)
-        return remote(w, w, rds.at[stream, t], rdr.at[stream, t], "dp", below)
-
-    def root_event(stream, k):
+        return remote(rl_v.at[pl.ds(0, rows)], rl_v.at[pl.ds(rows, rows)], rxs.at[0], rxr.at[0], "dp", partner)
+
+    def root_up(t):
+        return remote(root_rows(t), root_rows(t), rus.at[t], rur.at[t], "dp", above)
+
+    def root_down(t):
+        return remote(root_rows(t), root_rows(t), rds.at[t], rdr.at[t], "dp", below)
+
+    def root_event(k):
         if k == 0:
-            if stream == 1:
-                root_x().wait_recv()
-
             @pl.when(has_above)
             def _():
-                root_up(stream, z).start()
+                root_up(z).start()
 
             @pl.when(has_below)
             def _():
-                root_down(stream, z).start()
+                root_down(z).start()
             return
 
         @pl.when(z >= k)
         def _():
-            root_up(stream, z - k).wait_recv()
+            root_up(z - k).wait_recv()
 
             @pl.when(has_above)
             def _():
-                root_up(stream, z - k).start()
+                root_up(z - k).start()
 
         @pl.when(z + k < depth_z)
         def _():
-            root_down(stream, z + k).wait_recv()
+            root_down(z + k).wait_recv()
 
             @pl.when(has_below)
             def _():
-                root_down(stream, z + k).start()
+                root_down(z + k).start()
 
     for i in range(min(DEPTH, len(steps))):
         send_x(i).start()
-    for copy in loads_rr:
-        copy.wait()
-    root_event(0, 0)
+    load_rr.wait()
+    root_event(0)
     load_mine.wait()
-
-    events = {}
-    for k in range(1, depth_z):
-        events.setdefault(k - 1, []).append((0, k))
-    for k in range(depth_z):
-        events.setdefault(k + 1, []).append((1, k))
 
     for i, (s, h) in enumerate(steps):
         t = dest(s)
         send_x(i).wait_recv()
         if i + DEPTH < len(steps):
             send_x(i + DEPTH).start()
-        if i == 0:
+        if i == len(steps) - 1:
+            loads[0].wait()
             root_x().start()
         rs = sub(h)
         acc = mine[t, rs].astype(F32) + xbuf[t, rs].astype(F32)
@@ -220,11 +201,10 @@
             @pl.when(has_below)
             def _():
                 gat_down(z, h).start()
-        if h == halves - 1:
-            for event in events.pop(s, ()):
-                root_event(*event)
-
-    for copy in loads:
+        if h == halves - 1 and s < depth_z - 1:
+            root_event(s + 1)
+
+    for copy in loads[1:]:
         copy.wait()
     value = g[my_rows].astype(F32)
     one = 0.9 * first_v[...] + 0.1 * value
@@ -241,6 +221,42 @@
     stores[0].start()
     stores[1].start()
 
+    width = 256
+    pair_rows = 2 * rows
+    stepwise = pair_rows % LANES == 0
+
+    def tile_of(i):
+        return pl.ds(pl.multiple_of(i * width, width), width)
+
+    def absorb(t, begin):
+        for h in range(halves):
+            gat_x(t, h).wait_recv()
+        if not stepwise:
+            return
+        both = pl.ds(pl.multiple_of(t * pair_rows, pair_rows), pair_rows)
+
+        def step(i, carry):
+            c = tile_of(i)
+            more = jnp.dot(rl_v[:, both], g[both, c], preferred_element_type=F32)
+            inner[:, c] = more if begin else inner[:, c] + more
+            return carry
+
+        lax.fori_loop(0, size // width, step, 0)
+
+    def absorb_at(k):
+        if k == 0:
+            root_x().wait_recv()
+            absorb(z, True)
+            return
+
+        @pl.when(z >= k)
+        def _():
+            absorb(z - k, False)
+
+        @pl.when(z + k < depth_z)
+        def _():
+            absorb(z + k, False)
+
     for k in range(1, depth_z):
         for h in range(halves):
             @pl.when(z >= k)
@@ -260,40 +276,21 @@
                 @pl.when(has_below)
                 def _():
                     gat_down(z + k, h).start()
-        for event in events.pop(depth_z - 1 + k, ()):
-            root_event(*event)
-
-    def rebuild(i, carry):
-        r = pl.ds(pl.multiple_of(i * LANES, LANES), LANES)
-        for k in range(span):
-            c = pl.ds(pl.multiple_of(((i + k) % groups) * LANES, LANES), LANES)
-            piece = window[r, pl.ds(k * LANES, LANES)]
-            full[r, c] = piece
-            if k and 2 * k < groups:
-                full[c, r] = piece.T
-        return carry
-
-    lax.fori_loop(0, groups, rebuild, 0)
-
-    for t in range(depth_z):
-        for h in range(halves):
-            gat_x(t, h).wait_recv()
-
-    width = 256
-
-    def tile_of(i):
-        return pl.ds(pl.multiple_of(i * width, width), width)
-
-    def inner_step(i, carry):
-        c = tile_of(i)
-        inner[:, c] = jnp.dot(rl_v[...], g[:, c], preferred_element_type=F32).astype(BF16)
-        return carry
-
-    lax.fori_loop(0, size // width, inner_step, 0)
+        absorb_at(k - 1)
+    absorb_at(depth_z - 1)
+    if not stepwise:
+        def inner_step(i, carry):
+            c = tile_of(i)
+            inner[:, c] = jnp.dot(rl_v[...], g[:, c], preferred_element_type=F32)
+            return carry
+
+        lax.fori_loop(0, size // width, inner_step, 0)
 
     def parts_at(slot, cut):
-        w = size // cuts
-        return parts.at[slot, :, pl.ds(cut * w, w)]
+        return parts.at[slot, x if cut == 0 else 1 - x]
+
+    def swap():
+        return remote(away, parts.at[own, x], axs.at[0], axr.at[0], "dp", partner)
 
     def to_pair(k, cut):
         here = parts_at(own, cut)
@@ -304,17 +301,19 @@
         return remote(here, here, cs.at[k, cut], cr.at[k, cut], "own", pair * 2 + 1 - core)
 
     precond_sq = jnp.zeros((1, 1), F32)
-    for cut in range(cuts):
-        w = size // cuts
-        for j in range(w // width):
-            c = pl.ds(cut * w + j * width, width)
-            precond = jnp.dot(inner[...], full[:, c], preferred_element_type=F32)
-            parts[own, :, c] = precond.astype(BF16)
-            precond_sq += jnp.sum(
-                jnp.sum(precond * precond, axis=0, keepdims=True), axis=1, keepdims=True)
-        for k in range(1, pairs):
-            to_pair(k, cut).start()
-        to_core(0, cut).start()
+    rounded = inner[...].astype(BF16)
+    for j in range(size // 2 // width):
+        c = pl.ds(j * width, width)
+        precond = lax.dot_general(
+            rounded, right_rows[c, :], (((1,), (1,)), ((), ())), preferred_element_type=F32)
+        parts[own, x, :, c] = precond[:rows].astype(BF16)
+        away[:, c] = precond[rows:].astype(BF16)
+        precond_sq += jnp.sum(
+            jnp.sum(precond * precond, axis=0, keepdims=True), axis=1, keepdims=True)
+    swap().start()
+    for k in range(1, pairs):
+        to_pair(k, 0).start()
+    to_core(0, 0).start()
 
     line = lax.broadcasted_iota(jnp.int32, tile.shape, 0)
     tile[...] = jnp.where(line == 0, adam_sq, precond_sq)
@@ -325,6 +324,12 @@
 
     for k in range(1, n):
         norm_to(k).start()
+
+    def pass_half():
+        swap().wait_recv()
+        for k in range(1, pairs):
+            to_pair(k, 1).start()
+        to_core(0, 1).start()
 
     def left_step(i, carry):
         c = tile_of(i)
@@ -335,6 +340,7 @@
     lax.fori_loop(0, size // width, left_step, 0)
     stores[2].start()
 
+    pass_half()
     for k in range(1, n):
         norm_to(k).wait_recv()
     sums = stats[0]
@@ -379,7 +385,14 @@
         for k in range(pairs):
             to_core(k, cut).wait_recv()
     for b in range(owners):
-        direction[b] = (parts[owner[b]].astype(F32) * scales[owner[b]][0:1, 0:1]).astype(BF16)
+        factor = scales[owner[b]][0:1, 0:1]
+        for column in range(2):
+            scaled = (parts[owner[b], column].astype(F32) * factor).astype(BF16)
+            if rows % LANES:
+                direction[b, :, pl.ds(column * (size // 2), size // 2)] = scaled
+                continue
+            for t in range(depth_z):
+                direction[b, :, pl.ds((2 * t + column) * rows, rows)] = scaled[:, t * rows:(t + 1) * rows]
 
     for i, (s, h) in enumerate(steps):
         send_x(i).wait_send()
@@ -401,15 +414,15 @@
             @pl.when((z <= t) & has_below)
             def _():
                 gat_down(t, h).wait_send()
-        for stream in range(2):
-            @pl.when((z >= t) & has_above)
-            def _():
-                root_up(stream, t).wait_send()
-
-            @pl.when((z <= t) & has_below)
-            def _():
-                root_down(stream, t).wait_send()
+        @pl.when((z >= t) & has_above)
+        def _():
+            root_up(t).wait_send()
+
+        @pl.when((z <= t) & has_below)
+        def _():
+            root_down(t).wait_send()
     root_x().wait_send()
+    swap().wait_send()
     for k in range(1, n):
         norm_to(k).wait_send()
     for k in range(1, owners):
@@ -429,46 +442,50 @@
     halves = max(1, rows // 64)
     cuts = 2
     pairs = owners // 2
-    span = size // LANES // 2 + 1
     sem = pltpu.SemaphoreType.DMA
     stat = jax.ShapeDtypeStruct((1, rows, size), F32)
     anywhere = pl.BlockSpec(memory_space=pl.ANY)
-    return pl.pallas_call(
+    hbm = pl.BlockSpec(memory_space=pltpu.HBM)
+    *state, direction = pl.pallas_call(
         functools.partial(kernel, n, owners, halves, cuts),
         out_shape=(stat, stat, stat, stat, jax.ShapeDtypeStruct((owners, rows, size), BF16)),
-        in_specs=[anywhere] * 7 + [pl.BlockSpec(memory_space=pltpu.SMEM)],
+        in_specs=[hbm] * 7 + [pl.BlockSpec(memory_space=pltpu.SMEM)],
         out_specs=(anywhere,) * 4 + (pl.BlockSpec(memory_space=pltpu.VMEM),),
         scratch_shapes=[
             *[pltpu.VMEM((line, rows, size), BF16)] * 4,
             pltpu.VMEM((rows, size), F32),
             pltpu.VMEM((size, size), BF16),
-            pltpu.VMEM((size, span * LANES), BF16),
-            pltpu.VMEM((size, size), BF16),
+            pltpu.VMEM((size // 2, size), BF16),
             pltpu.VMEM((rows, size), F32),
             pltpu.VMEM((rows, size), F32),
-            pltpu.VMEM((rows, size), BF16),
+            pltpu.VMEM((2 * rows, size), BF16),
             pltpu.VMEM((rows, size), F32),
             pltpu.VMEM((rows, size), F32),
-            pltpu.VMEM((rows, size), BF16),
+            pltpu.VMEM((2 * rows, size), F32),
             pltpu.VMEM((LANES, size), BF16),
             pltpu.VMEM((LANES, 256), F32),
-            pltpu.VMEM((owners, rows, size), BF16),
+            pltpu.VMEM((owners, 2, rows, size // 2), BF16),
+            pltpu.VMEM((rows, size // 2), BF16),
             pltpu.VMEM((8, LANES), F32),
             pltpu.VMEM((n, 8, LANES), F32),
             pltpu.VMEM((owners, 8, LANES), F32),
-            sem((6 + span,)), sem((4,)),
+            sem((7,)), sem((4,)),
             sem((line * halves,)), sem((line * halves,)),
             *[sem((line, halves))] * 10,
             sem((1,)), sem((1,)),
-            *[sem((2, line))] * 4,
+            *[sem((line,))] * 4,
+            sem((1,)), sem((1,)),
             *[sem((pairs, cuts))] * 4,
             sem((n,)), sem((n,)), sem((owners,)), sem((owners,)),
         ],
         compiler_params=pltpu.CompilerParams(
-            collective_id=0, has_side_effects=True, vmem_limit_bytes=40 * 1024 * 1024),
+            collective_id=0, has_side_effects=True, vmem_limit_bytes=60 * 1024 * 1024),
         cost_estimate=pl.CostEstimate(
             flops=8 * rows * size * size, bytes_accessed=24 * rows * size, transcendentals=rows * size),
     )(grads.reshape(line, 2, rows, size), left, right, root_left, root_right, first, second, owner)
+    if rows % LANES:
+        direction = direction.reshape(owners, rows, 2, line, rows).swapaxes(2, 3).reshape(owners, rows, size)
+    return (*state, direction)
 
 
 def solution(mesh):

time: 92.5 us -> 88.3 us (0.955)
  local copies, waits for them, and re-layouts: 12.4 us -> 6.48 us
  Pallas kernels: 78.9 us -> 81 us
    unnamed x21 -> x11, local copies, waits for them, and re-layouts: 12.4 us -> 6.48 us
    pallas_call x1, Pallas kernels: 78.9 us -> 81 us  [body(): pl.pallas_call(functools.partial(kernel, n, owners, halves, cuts), out_sh...]
where the time goes in v2:
time: 88.3 us; the launch traced here: 88.1 us
  Pallas kernels  81 us (92%)
  local copies, waits for them, and re-layouts  6.48 us (7%)
    pallas_call x1, Pallas kernels, body(): pl.pallas_call(functools.partial(kernel, n, owners, halves, cuts), out_sh...  81 us
    unnamed x11, local copies, waits for them, and re-layouts  6.48 us

profile of v2, /device:TPU:0, one launch (start us, length us, event | category | flops | bytes accessed | tf_op | source)
XLA Modules:
  0.0 88.1 jit_solution(8071565192080428298)
XLA Ops:
  0.6 81.0 %shard_map.119 = (f32[1,128,1024]{2,1,0:T(8,128)}, f32[1,128,1024]{2,1,0:T(8,128)}, f32[1,128,1024]{2,1,0:T(8,128)}, f32[1,128,1024]{2,1,0:T(8,128)}, bf16[4,128,1024]{2,1,0:T(8,128)(2,1)}) custom-call(bf16[4,2,128,1024]{3,2,1,0:T(8,128)(2,1)} %bitcast.1, f32[1,128,1024]{2,1,0:T(8,128)} %left.1, f32[1,128,1024]{2,1,0:T(8,128)} %right.1, ...), custom_call_target="tpu_custom_call" | custom-call | flops 1073741824 | bytes 3145728 | tf_op jit(solution)/shard_map/pallas_call | solution.py:449
  81.6 0.0 copy-start.2
  81.6 0.0 copy-start.1
  81.6 0.0 copy-start
  81.6 2.0 %copy.18 = f32[1,128,1024]{2,1,0:T(8,128)} copy(f32[1,128,1024]{2,1,0:T(8,128)} %get-tuple-element.10) | data formatting | bytes 1048576
  83.7 1.9 %copy.19 = f32[1,128,1024]{2,1,0:T(8,128)} copy(f32[1,128,1024]{2,1,0:T(8,128)} %get-tuple-element.11) | data formatting | bytes 1048576
  85.5 0.0 copy-done.2
  85.5 0.8 copy.20
  86.3 0.0 copy-done.1
  86.3 0.8 copy.21
  87.1 0.0 copy-done
  87.1 1.0 %copy.22 = bf16[4,128,1024]{2,1,0:T(8,128)(2,1)} copy(bf16[4,128,1024]{2,1,0:T(8,128)(2,1)S(1)} %copy-done) | data formatting | bytes 2097152
Async XLA Ops:
  81.6 3.9 %copy-start.2 = (f32[1,128,1024]{2,1,0:T(8,128)S(1)}, f32[1,128,1024]{2,1,0:T(8,128)}, u32[]{:S(2)}) copy-start(f32[1,128,1024]{2,1,0:T(8,128)} %get-tuple-element.12) | copy-start | bytes 1572868
  81.6 4.7 %copy-start.1 = (f32[1,128,1024]{2,1,0:T(8,128)S(1)}, f32[1,128,1024]{2,1,0:T(8,128)}, u32[]{:S(2)}) copy-start(f32[1,128,1024]{2,1,0:T(8,128)} %get-tuple-element.13) | copy-start | bytes 1572868
  81.6 5.5 %copy-start = (bf16[4,128,1024]{2,1,0:T(8,128)(2,1)S(1)}, bf16[4,128,1024]{2,1,0:T(8,128)(2,1)}, u32[]{:S(2)}) copy-start(bf16[4,128,1024]{2,1,0:T(8,128)(2,1)} %get-tuple-element.14) | copy-start | bytes 3145732

commit v3 on v2

--- a/solution.py
+++ b/solution.py
@@ -12,6 +12,7 @@
 BF16 = jnp.bfloat16
 LANES = 128
 DEPTH = 3
+VMEM = 60 * 1024 * 1024
 
 
 def remote(src, dst, send, recv, axis, to):
@@ -201,8 +202,8 @@
             @pl.when(has_below)
             def _():
                 gat_down(z, h).start()
-        if h == halves - 1 and s < depth_z - 1:
-            root_event(s + 1)
+        if h == halves - 1 and 0 < s < depth_z - 1:
+            root_event(s)
 
     for copy in loads[1:]:
         copy.wait()
@@ -277,6 +278,8 @@
                 def _():
                     gat_down(z + k, h).start()
         absorb_at(k - 1)
+        if k == max(1, depth_z - 2):
+            root_event(depth_z - 1)
     absorb_at(depth_z - 1)
     if not stepwise:
         def inner_step(i, carry):
@@ -434,6 +437,35 @@
                 to_pair(k, cut).wait_send()
     for copy in stores:
         copy.wait()
+
+
+def finish_kernel(*refs):
+    count = len(refs) // 2
+    sources, targets, sem = refs[:count], refs[count:2 * count], refs[2 * count]
+    copies = []
+    for source, target in zip(sources, targets):
+        blocks, rows, _ = source.shape
+        cut = rows // 2 if blocks == 1 else rows
+        for b in range(blocks):
+            for at in range(0, rows, cut):
+                piece = (b, pl.ds(at, cut))
+                copies.append(pltpu.make_async_copy(source.at[piece], target.at[piece], sem.at[len(copies)]))
+    for copy in copies:
+        copy.start()
+    for copy in copies:
+        copy.wait()
+
+
+def finish(*arrays):
+    anywhere = pl.BlockSpec(memory_space=pl.ANY)
+    return pl.pallas_call(
+        finish_kernel,
+        out_shape=tuple(jax.ShapeDtypeStruct(a.shape, a.dtype) for a in arrays),
+        in_specs=[anywhere] * len(arrays),
+        out_specs=(anywhere,) * len(arrays),
+        scratch_shapes=[pltpu.SemaphoreType.DMA((sum(max(2, a.shape[0]) for a in arrays),))],
+        compiler_params=pltpu.CompilerParams(vmem_limit_bytes=VMEM),
+    )(*arrays)
 
 
 def body(n, owners, grads, left, right, root_left, root_right, first, second, owner):
@@ -479,13 +511,13 @@
             sem((n,)), sem((n,)), sem((owners,)), sem((owners,)),
         ],
         compiler_params=pltpu.CompilerParams(
-            collective_id=0, has_side_effects=True, vmem_limit_bytes=60 * 1024 * 1024),
+            collective_id=0, has_side_effects=True, vmem_limit_bytes=VMEM),
         cost_estimate=pl.CostEstimate(
             flops=8 * rows * size * size, bytes_accessed=24 * rows * size, transcendentals=rows * size),
     )(grads.reshape(line, 2, rows, size), left, right, root_left, root_right, first, second, owner)
     if rows % LANES:
         direction = direction.reshape(owners, rows, 2, line, rows).swapaxes(2, 3).reshape(owners, rows, size)
-    return (*state, direction)
+    return finish(*state, direction)
 
 
 def solution(mesh):

time: 88.3 us -> 176 us (1.99)
  Pallas kernels: 81 us -> 176 us
  local copies, waits for them, and re-layouts: 6.48 us -> 0 us
    pallas_call x0 -> x1, Pallas kernels: none -> 96.5 us  [finish(): pl.pallas_call(finish_kernel, out_shape=tuple((jax.ShapeDtypeStruct(a.sha...]
    unnamed x11 -> x0, local copies, waits for them, and re-layouts: 6.48 us -> none
    pallas_call x1, Pallas kernels: 81 us -> 79.1 us  [body(): pl.pallas_call(functools.partial(kernel, n, owners, halves, cuts), out_sh...]
where the time goes in v3:
time: 176 us
  Pallas kernels  176 us (100%)
    pallas_call x1, Pallas kernels, finish(): pl.pallas_call(finish_kernel, out_shape=tuple((jax.ShapeDtypeStruct(a.sha...  96.5 us
    pallas_call x1, Pallas kernels, body(): pl.pallas_call(functools.partial(kernel, n, owners, halves, cuts), out_sh...  79.1 us

profile of v3, /device:TPU:0, one launch (start us, length us, event | category | flops | bytes accessed | tf_op | source)
XLA Modules:
  0.0 176.3 jit_solution(17695050825974243206)
XLA Ops:
  0.6 79.1 %shard_map.119 = (f32[1,128,1024]{2,1,0:T(8,128)}, f32[1,128,1024]{2,1,0:T(8,128)}, f32[1,128,1024]{2,1,0:T(8,128)}, f32[1,128,1024]{2,1,0:T(8,128)}, bf16[4,128,1024]{2,1,0:T(8,128)(2,1)}) custom-call(bf16[4,2,128,1024]{3,2,1,0:T(8,128)(2,1)} %bitcast.1, f32[1,128,1024]{2,1,0:T(8,128)} %left.1, f32[1,128,1024]{2,1,0:T(8,128)} %right.1, ...), custom_call_target="tpu_custom_call" | custom-call | flops 1073741824 | bytes 3145728 | tf_op jit(solution)/shard_map/pallas_call | solution.py:481
  79.8 96.5 %shard_map.120 = (f32[1,128,1024]{2,1,0:T(8,128)}, f32[1,128,1024]{2,1,0:T(8,128)}, f32[1,128,1024]{2,1,0:T(8,128)}, f32[1,128,1024]{2,1,0:T(8,128)}, bf16[4,128,1024]{2,1,0:T(8,128)(2,1)}) custom-call(f32[1,128,1024]{2,1,0:T(8,128)} %get-tuple-element.10.refs_0_, f32[1,128,1024]{2,1,0:T(8,128)} %get-tuple-element.11.refs_1_, ...), custom_call_target="tpu_custom_call" | custom-call | tf_op jit(solution)/shard_map/pallas_call | solution.py:461

commit v4 on v3

--- a/solution.py
+++ b/solution.py
@@ -202,8 +202,8 @@
             @pl.when(has_below)
             def _():
                 gat_down(z, h).start()
-        if h == halves - 1 and 0 < s < depth_z - 1:
-            root_event(s)
+        if h == halves - 1 and s < (depth_z - 1) // 2:
+            root_event(s + 1)
 
     for copy in loads[1:]:
         copy.wait()
@@ -278,9 +278,12 @@
                 def _():
                     gat_down(z + k, h).start()
         absorb_at(k - 1)
-        if k == max(1, depth_z - 2):
-            root_event(depth_z - 1)
+        late = (depth_z - 1) // 2 + k
+        if late < depth_z - 1:
+            root_event(late)
     absorb_at(depth_z - 1)
+    if depth_z > 1:
+        root_event(depth_z - 1)
     if not stepwise:
         def inner_step(i, carry):
             c = tile_of(i)
@@ -439,31 +442,40 @@
         copy.wait()
 
 
-def finish_kernel(*refs):
-    count = len(refs) // 2
-    sources, targets, sem = refs[:count], refs[count:2 * count], refs[2 * count]
+def finish_kernel(count, *refs):
+    sources, targets, holds = refs[:count], refs[count:2 * count], refs[2 * count:3 * count]
+    in_sem, out_sem = refs[3 * count:]
     copies = []
-    for source, target in zip(sources, targets):
+    for source, target, hold in zip(sources, targets, holds):
         blocks, rows, _ = source.shape
         cut = rows // 2 if blocks == 1 else rows
         for b in range(blocks):
             for at in range(0, rows, cut):
                 piece = (b, pl.ds(at, cut))
-                copies.append(pltpu.make_async_copy(source.at[piece], target.at[piece], sem.at[len(copies)]))
-    for copy in copies:
-        copy.start()
-    for copy in copies:
-        copy.wait()
+                i = len(copies)
+                copies.append((
+                    pltpu.make_async_copy(source.at[piece], hold.at[piece], in_sem.at[i]),
+                    pltpu.make_async_copy(hold.at[piece], target.at[piece], out_sem.at[i])))
+    for load, _ in copies:
+        load.start()
+    for load, store in copies:
+        load.wait()
+        store.start()
+    for _, store in copies:
+        store.wait()
 
 
 def finish(*arrays):
+    count = len(arrays)
+    pieces = sum(max(2, a.shape[0]) for a in arrays)
     anywhere = pl.BlockSpec(memory_space=pl.ANY)
     return pl.pallas_call(
-        finish_kernel,
+        functools.partial(finish_kernel, count),
         out_shape=tuple(jax.ShapeDtypeStruct(a.shape, a.dtype) for a in arrays),
-        in_specs=[anywhere] * len(arrays),
-        out_specs=(anywhere,) * len(arrays),
-        scratch_shapes=[pltpu.SemaphoreType.DMA((sum(max(2, a.shape[0]) for a in arrays),))],
+        in_specs=[anywhere] * count,
+        out_specs=(anywhere,) * count,
+        scratch_shapes=[pltpu.VMEM(a.shape, a.dtype) for a in arrays]
+        + [pltpu.SemaphoreType.DMA((pieces,))] * 2,
         compiler_params=pltpu.CompilerParams(vmem_limit_bytes=VMEM),
     )(*arrays)
 

time: 176 us -> 79.4 us (0.45)
  Pallas kernels: 176 us -> 78.6 us
    pallas_call x1, Pallas kernels: 96.5 us -> 2.81 us  [finish(): pl.pallas_call(functools.partial(finish_kernel, count), out_shape=tuple((...]
    pallas_call x1, Pallas kernels: 79.1 us -> 75.8 us  [body(): pl.pallas_call(functools.partial(kernel, n, owners, halves, cuts), out_sh...]
where the time goes in v4:
time: 79.4 us; the launch traced here: 79.2 us
  Pallas kernels  78.6 us (99%)
    pallas_call x1, Pallas kernels, body(): pl.pallas_call(functools.partial(kernel, n, owners, halves, cuts), out_sh...  75.8 us
    pallas_call x1, Pallas kernels, finish(): pl.pallas_call(functools.partial(finish_kernel, count), out_shape=tuple((...  2.81 us

profile of v4, /device:TPU:0, one launch (start us, length us, event | category | flops | bytes accessed | tf_op | source)
XLA Modules:
  0.0 79.2 jit_solution(12534515018184994172)
XLA Ops:
  0.6 75.8 %shard_map.119 = (f32[1,128,1024]{2,1,0:T(8,128)}, f32[1,128,1024]{2,1,0:T(8,128)}, f32[1,128,1024]{2,1,0:T(8,128)}, f32[1,128,1024]{2,1,0:T(8,128)}, bf16[4,128,1024]{2,1,0:T(8,128)(2,1)}) custom-call(bf16[4,2,128,1024]{3,2,1,0:T(8,128)(2,1)} %bitcast.1, f32[1,128,1024]{2,1,0:T(8,128)} %left.1, f32[1,128,1024]{2,1,0:T(8,128)} %right.1, ...), custom_call_target="tpu_custom_call" | custom-call | flops 1073741824 | bytes 3145728 | tf_op jit(solution)/shard_map/pallas_call | solution.py:493
  76.4 2.8 %shard_map.120 = (f32[1,128,1024]{2,1,0:T(8,128)}, f32[1,128,1024]{2,1,0:T(8,128)}, f32[1,128,1024]{2,1,0:T(8,128)}, f32[1,128,1024]{2,1,0:T(8,128)}, bf16[4,128,1024]{2,1,0:T(8,128)(2,1)}) custom-call(f32[1,128,1024]{2,1,0:T(8,128)} %get-tuple-element.10.refs_0_, f32[1,128,1024]{2,1,0:T(8,128)} %get-tuple-element.11.refs_1_, ...), custom_call_target="tpu_custom_call" | custom-call | tf_op jit(solution)/shard_map/pallas_call | solution.py:472

commit v5 on v4

--- a/solution.py
+++ b/solution.py
@@ -24,10 +24,11 @@
 
 def kernel(n, owners, halves, cuts, grads, left, right, root_left, root_right, first, second, owner,
            new_left, new_right, new_first, new_second, direction,
-           mine, xbuf, ubuf, dbuf, total, g, right_rows, left_v, right_v, rl_v, first_v, second_v,
+           mine, xbuf, ubuf, dbuf, tmine, tub, tdb, tx, total, g, right_rows, left_v, right_v, rl_v, first_v, second_v,
            inner, turned, product, parts, away, tile, stats, scales,
            load_sem, store_sem, xs, xr, us, ur, ds, dr, gxs, gxr, gus, gur, gds, gdr,
-           rxs, rxr, rus, rur, rds, rdr, axs, axr, ps, pr, cs, cr, ss, sr, ts, tr):
+           rxs, rxr, rus, rur, rds, rdr, axs, axr, ps, pr, cs, cr, ss, sr, ts, tr,
+           tus, tur, tds, tdr, txs, txr, hxs, hxr, hus, hur, hds, hdr):
     me = lax.axis_index("dp")
     own = lax.axis_index("own")
     size = g.shape[0]
@@ -41,6 +42,8 @@
     groups = size // LANES
     has_above, has_below = z < depth_z - 1, z > 0
 
+    head, tail = pl.ds(0, size - LANES), pl.ds(size - LANES, LANES)
+
     def root_rows(t):
         return right_rows.at[pl.ds(pl.multiple_of(t * rows, rows), rows)]
 
@@ -54,7 +57,9 @@
     group = (me * rows) // LANES
     load_rr = pltpu.make_async_copy(root_right.at[0], root_rows(z), load_sem.at[6])
     load_rr.start()
+    load_tail = pltpu.make_async_copy(grads.at[:, 1 - x, :, tail], tmine, load_sem.at[7])
     load_mine.start()
+    load_tail.start()
     for copy in loads:
         copy.start()
 
@@ -83,7 +88,7 @@
     def send_x(i):
         s, h = steps[i]
         t = dest(s)
-        return remote(grads.at[t, 1 - x, sub(h)], xbuf.at[t, sub(h)], xs.at[i], xr.at[i], "dp", partner)
+        return remote(grads.at[t, 1 - x, sub(h), head], xbuf.at[t, sub(h), head], xs.at[i], xr.at[i], "dp", partner)
 
     def send_up(t, h):
         return remote(mine.at[t, sub(h)], ubuf.at[t, sub(h)], us.at[t, h], ur.at[t, h], "dp", above)
@@ -91,11 +96,97 @@
     def send_down(t, h):
         return remote(mine.at[t, sub(h)], dbuf.at[t, sub(h)], ds.at[t, h], dr.at[t, h], "dp", below)
 
+    def tail_up(t):
+        return remote(tmine.at[t], tub.at[t], tus.at[t], tur.at[t], "dp", above)
+
+    def tail_down(t):
+        return remote(tmine.at[t], tdb.at[t], tds.at[t], tdr.at[t], "dp", below)
+
+    def tail_x():
+        return remote(tmine.at[z], tx, txs.at[0], txr.at[0], "dp", partner)
+
+    def tail_step(s):
+        t = dest(s)
+        if s < depth_z - 1:
+            @pl.when((t > z) & has_below)
+            def _():
+                tail_up(t).wait_recv()
+                tmine[t] = (tmine[t].astype(F32) + tub[t].astype(F32)).astype(BF16)
+
+            @pl.when((t < z) & has_above)
+            def _():
+                tail_down(t).wait_recv()
+                tmine[t] = (tmine[t].astype(F32) + tdb[t].astype(F32)).astype(BF16)
+
+            @pl.when(t > z)
+            def _():
+                tail_up(t).start()
+
+            @pl.when(t < z)
+            def _():
+                tail_down(t).start()
+            return
+
+        @pl.when(has_below)
+        def _():
+            tail_up(z).wait_recv()
+            tmine[z] = (tmine[z].astype(F32) + tub[z].astype(F32)).astype(BF16)
+
+        @pl.when(has_above)
+        def _():
+            tail_down(z).wait_recv()
+            tmine[z] = (tmine[z].astype(F32) + tdb[z].astype(F32)).astype(BF16)
+
+        tail_x().start()
+
     def block(t, column, h):
         return g.at[pl.ds(pl.multiple_of((2 * t + column) * rows + h * part, part), part)]
 
     def gat_x(t, h):
-        return remote(block(t, x, h), block(t, x, h), gxs.at[t, h], gxr.at[t, h], "dp", partner)
+        here = block(t, x, h).at[:, head]
+        return remote(here, here, gxs.at[t, h], gxr.at[t, h], "dp", partner)
+
+    def end_x(h):
+        here = block(z, x, h).at[:, tail]
+        return remote(here, here, hxs.at[h], hxr.at[h], "dp", partner)
+
+    def end_up(t, h):
+        here = block(t, 1 - x, h).at[:, tail]
+        return remote(here, here, hus.at[t, h], hur.at[t, h], "dp", above)
+
+    def end_down(t, h):
+        here = block(t, 1 - x, h).at[:, tail]
+        return remote(here, here, hds.at[t, h], hdr.at[t, h], "dp", below)
+
+    def end_event(k):
+        for h in range(halves):
+            if k == 0:
+                end_x(h).wait_recv()
+
+                @pl.when(has_above)
+                def _():
+                    end_up(z, h).start()
+
+                @pl.when(has_below)
+                def _():
+                    end_down(z, h).start()
+                continue
+
+            @pl.when(z >= k)
+            def _():
+                end_up(z - k, h).wait_recv()
+
+                @pl.when(has_above)
+                def _():
+                    end_up(z - k, h).start()
+
+            @pl.when(z + k < depth_z)
+            def _():
+                end_down(z + k, h).wait_recv()
+
+                @pl.when(has_below)
+                def _():
+                    end_down(z + k, h).start()
 
     def gat_up(t, h):
         return remote(block(t, x, h), block(t, x, h), gus.at[t, h], gur.at[t, h], "dp", above)
@@ -143,10 +234,14 @@
         send_x(i).start()
     load_rr.wait()
     root_event(0)
+    xbuf[:, :, tail] = jnp.zeros((depth_z, rows, LANES), BF16)
     load_mine.wait()
+    load_tail.wait()
 
     for i, (s, h) in enumerate(steps):
         t = dest(s)
+        if h == 0:
+            tail_step(s)
         send_x(i).wait_recv()
         if i + DEPTH < len(steps):
             send_x(i + DEPTH).start()
@@ -192,7 +287,11 @@
                 send_down(t, h).wait_recv()
                 total[rs] = total[rs] + dbuf[t, rs].astype(F32)
 
+            if h == 0:
+                tail_x().wait_recv()
+            total[rs, tail] = total[rs, tail] + tx[rs].astype(F32)
             g[pl.ds(pl.multiple_of(me * rows + h * part, part), part)] = (total[rs] / n).astype(BF16)
+            end_x(h).start()
             gat_x(z, h).start()
 
             @pl.when(has_above)
@@ -258,6 +357,7 @@
         def _():
             absorb(z + k, False)
 
+    end_event(0)
     for k in range(1, depth_z):
         for h in range(halves):
             @pl.when(z >= k)
@@ -277,6 +377,7 @@
                 @pl.when(has_below)
                 def _():
                     gat_down(z + k, h).start()
+        end_event(k)
         absorb_at(k - 1)
         late = (depth_z - 1) // 2 + k
         if late < depth_z - 1:
@@ -405,6 +506,14 @@
         gat_x(s, h).wait_send()
     for t in range(depth_z):
         for h in range(halves):
+            @pl.when((z >= t) & has_above)
+            def _():
+                end_up(t, h).wait_send()
+
+            @pl.when((z <= t) & has_below)
+            def _():
+                end_down(t, h).wait_send()
+
             @pl.when(z < t)
             def _():
                 send_up(t, h).wait_send()
@@ -420,6 +529,14 @@
             @pl.when((z <= t) & has_below)
             def _():
                 gat_down(t, h).wait_send()
+        @pl.when(z < t)
+        def _():
+            tail_up(t).wait_send()
+
+        @pl.when(z > t)
+        def _():
+            tail_down(t).wait_send()
+
         @pl.when((z >= t) & has_above)
         def _():
             root_up(t).wait_send()
@@ -428,6 +545,9 @@
         def _():
             root_down(t).wait_send()
     root_x().wait_send()
+    tail_x().wait_send()
+    for h in range(halves):
+        end_x(h).wait_send()
     swap().wait_send()
     for k in range(1, n):
         norm_to(k).wait_send()
@@ -497,6 +617,8 @@
         out_specs=(anywhere,) * 4 + (pl.BlockSpec(memory_space=pltpu.VMEM),),
         scratch_shapes=[
             *[pltpu.VMEM((line, rows, size), BF16)] * 4,
+            *[pltpu.VMEM((line, rows, LANES), BF16)] * 3,
+            pltpu.VMEM((rows, LANES), BF16),
             pltpu.VMEM((rows, size), F32),
             pltpu.VMEM((size, size), BF16),
             pltpu.VMEM((size // 2, size), BF16),
@@ -513,7 +635,7 @@
             pltpu.VMEM((8, LANES), F32),
             pltpu.VMEM((n, 8, LANES), F32),
             pltpu.VMEM((owners, 8, LANES), F32),
-            sem((7,)), sem((4,)),
+            sem((8,)), sem((4,)),
             sem((line * halves,)), sem((line * halves,)),
             *[sem((line, halves))] * 10,
             sem((1,)), sem((1,)),
@@ -521,6 +643,9 @@
             sem((1,)), sem((1,)),
             *[sem((pairs, cuts))] * 4,
             sem((n,)), sem((n,)), sem((owners,)), sem((owners,)),
+            *[sem((line,))] * 4,
+            sem((1,)), sem((1,)), sem((halves,)), sem((halves,)),
+            *[sem((line, halves))] * 4,
         ],
         compiler_params=pltpu.CompilerParams(
             collective_id=0, has_side_effects=True, vmem_limit_bytes=VMEM),

time: 79.4 us -> 82.9 us (1.044)
  Pallas kernels: 78.6 us -> 82.1 us
    pallas_call x1, Pallas kernels: 75.8 us -> 79.3 us  [body(): pl.pallas_call(functools.partial(kernel, n, owners, halves, cuts), out_sh...]
where the time goes in v5:
time: 82.9 us; the launch traced here: 82.8 us
  Pallas kernels  82.1 us (99%)
    pallas_call x1, Pallas kernels, body(): pl.pallas_call(functools.partial(kernel, n, owners, halves, cuts), out_sh...  79.3 us
    pallas_call x1, Pallas kernels, finish(): pl.pallas_call(functools.partial(finish_kernel, count), out_shape=tuple((...  2.81 us

profile of v5, /device:TPU:0, one launch (start us, length us, event | category | flops | bytes accessed | tf_op | source)
XLA Modules:
  0.0 82.8 jit_solution(11072601457854472119)
XLA Ops:
  0.6 79.3 %shard_map.119 = (f32[1,128,1024]{2,1,0:T(8,128)}, f32[1,128,1024]{2,1,0:T(8,128)}, f32[1,128,1024]{2,1,0:T(8,128)}, f32[1,128,1024]{2,1,0:T(8,128)}, bf16[4,128,1024]{2,1,0:T(8,128)(2,1)}) custom-call(bf16[4,2,128,1024]{3,2,1,0:T(8,128)(2,1)} %bitcast.1, f32[1,128,1024]{2,1,0:T(8,128)} %left.1, f32[1,128,1024]{2,1,0:T(8,128)} %right.1, ...), custom_call_target="tpu_custom_call" | custom-call | flops 1073741824 | bytes 3145728 | tf_op jit(solution)/shard_map/pallas_call | solution.py:613
  80.0 2.8 %shard_map.120 = (f32[1,128,1024]{2,1,0:T(8,128)}, f32[1,128,1024]{2,1,0:T(8,128)}, f32[1,128,1024]{2,1,0:T(8,128)}, f32[1,128,1024]{2,1,0:T(8,128)}, bf16[4,128,1024]{2,1,0:T(8,128)(2,1)}) custom-call(f32[1,128,1024]{2,1,0:T(8,128)} %get-tuple-element.10.refs_0_, f32[1,128,1024]{2,1,0:T(8,128)} %get-tuple-element.11.refs_1_, ...), custom_call_target="tpu_custom_call" | custom-call | tf_op jit(solution)/shard_map/pallas_call | solution.py:592

commit v6 on v4

--- a/solution.py
+++ b/solution.py
@@ -25,7 +25,7 @@
 def kernel(n, owners, halves, cuts, grads, left, right, root_left, root_right, first, second, owner,
            new_left, new_right, new_first, new_second, direction,
            mine, xbuf, ubuf, dbuf, total, g, right_rows, left_v, right_v, rl_v, first_v, second_v,
-           inner, turned, product, parts, away, tile, stats, scales,
+           inner, turned, product, parts, scaled_v, away, tile, stats, scales,
            load_sem, store_sem, xs, xr, us, ur, ds, dr, gxs, gxr, gus, gur, gds, gdr,
            rxs, rxr, rus, rur, rds, rdr, axs, axr, ps, pr, cs, cr, ss, sr, ts, tr):
     me = lax.axis_index("dp")
@@ -395,10 +395,12 @@
         for column in range(2):
             scaled = (parts[owner[b], column].astype(F32) * factor).astype(BF16)
             if rows % LANES:
-                direction[b, :, pl.ds(column * (size // 2), size // 2)] = scaled
+                scaled_v[b, :, pl.ds(column * (size // 2), size // 2)] = scaled
                 continue
             for t in range(depth_z):
-                direction[b, :, pl.ds((2 * t + column) * rows, rows)] = scaled[:, t * rows:(t + 1) * rows]
+                scaled_v[b, :, pl.ds((2 * t + column) * rows, rows)] = scaled[:, t * rows:(t + 1) * rows]
+        stores.append(pltpu.make_async_copy(scaled_v.at[b], direction.at[b], store_sem.at[4 + b]))
+        stores[-1].start()
 
     for i, (s, h) in enumerate(steps):
         send_x(i).wait_send()
@@ -494,7 +496,7 @@
         functools.partial(kernel, n, owners, halves, cuts),
         out_shape=(stat, stat, stat, stat, jax.ShapeDtypeStruct((owners, rows, size), BF16)),
         in_specs=[hbm] * 7 + [pl.BlockSpec(memory_space=pltpu.SMEM)],
-        out_specs=(anywhere,) * 4 + (pl.BlockSpec(memory_space=pltpu.VMEM),),
+        out_specs=(anywhere,) * 5,
         scratch_shapes=[
             *[pltpu.VMEM((line, rows, size), BF16)] * 4,
             pltpu.VMEM((rows, size), F32),
@@ -509,11 +511,12 @@
             pltpu.VMEM((LANES, size), BF16),
             pltpu.VMEM((LANES, 256), F32),
             pltpu.VMEM((owners, 2, rows, size // 2), BF16),
+            pltpu.VMEM((owners, rows, size), BF16),
             pltpu.VMEM((rows, size // 2), BF16),
             pltpu.VMEM((8, LANES), F32),
             pltpu.VMEM((n, 8, LANES), F32),
             pltpu.VMEM((owners, 8, LANES), F32),
-            sem((7,)), sem((4,)),
+            sem((7,)), sem((4 + owners,)),
             sem((line * halves,)), sem((line * halves,)),
             *[sem((line, halves))] * 10,
             sem((1,)), sem((1,)),

time: 79.4 us -> 78.8 us (level)
  no operation moved by 1% of the time
where the time goes in v6:
time: 78.8 us; the launch traced here: 78.7 us
  Pallas kernels  78 us (99%)
    pallas_call x1, Pallas kernels, body(): pl.pallas_call(functools.partial(kernel, n, owners, halves, cuts), out_sh...  75.2 us
    pallas_call x1, Pallas kernels, finish(): pl.pallas_call(functools.partial(finish_kernel, count), out_shape=tuple((...  2.81 us

profile of v6, /device:TPU:0, one launch (start us, length us, event | category | flops | bytes accessed | tf_op | source)
XLA Modules:
  0.0 78.7 jit_solution(17486401052649536133)
XLA Ops:
  0.6 75.2 %shard_map.119 = (f32[1,128,1024]{2,1,0:T(8,128)}, f32[1,128,1024]{2,1,0:T(8,128)}, f32[1,128,1024]{2,1,0:T(8,128)}, f32[1,128,1024]{2,1,0:T(8,128)}, bf16[4,128,1024]{2,1,0:T(8,128)(2,1)}) custom-call(bf16[4,2,128,1024]{3,2,1,0:T(8,128)(2,1)} %bitcast.1, f32[1,128,1024]{2,1,0:T(8,128)} %left.1, f32[1,128,1024]{2,1,0:T(8,128)} %right.1, ...), custom_call_target="tpu_custom_call" | custom-call | flops 1073741824 | bytes 3145728 | tf_op jit(solution)/shard_map/pallas_call | solution.py:495
  75.8 2.8 %shard_map.120 = (f32[1,128,1024]{2,1,0:T(8,128)}, f32[1,128,1024]{2,1,0:T(8,128)}, f32[1,128,1024]{2,1,0:T(8,128)}, f32[1,128,1024]{2,1,0:T(8,128)}, bf16[4,128,1024]{2,1,0:T(8,128)(2,1)}) custom-call(f32[1,128,1024]{2,1,0:T(8,128)} %get-tuple-element.10.refs_0_, f32[1,128,1024]{2,1,0:T(8,128)} %get-tuple-element.11.refs_1_, ...), custom_call_target="tpu_custom_call" | custom-call | tf_op jit(solution)/shard_map/pallas_call | solution.py:474
